TPU v7x, 32 devices: a whole 2x2x4 slice. The times are simulated.
32 devices in a mesh: grp: 4 (over y, x), cell: 8 (over z, core).
Axes of the slice: x: 2, y: 2, z: 4, core: 2. Of those that a mesh axis runs over, the one named last changes fastest.
Arguments:
- occurrence: bfloat16 [98304, 4096], P(('grp', 'cell')), may hold values from 0 to 1, as said below
- condition: bfloat16 [98304], P(('grp', 'cell')), may hold values from 0.05 to 1, as said below
- neighbours: int32 [768, 4], P(('grp', 'cell')), may hold values from 0 to 767, as said below
- pair_count: int32 [768], P(('grp', 'cell')), may hold values from 0 to 4
Outputs:
- effective: float32 [98304], P(('grp', 'cell'))
- persistence: float32 [4096], P(('grp', 'cell'))
Inputs may be any that keep to these rules, and one draw needn't show every extreme that they name: occurrence probabilities, positive. habitat condition, positive. `neighbours`: entry k of row t, for k < pair_count[t], is a tile u != t with |u - t| <= 2 in the same band of 192 consecutive tiles (t // 192 == u // 192); entries are distinct; pairing is symmetric (u lists t whenever t lists u); later entries hold t.
All inputs are finite; a program needn't handle non-finite values.
Results may differ from a plain program's by a relative error of at most 0.0003.
Values may be sent and summed in bfloat16 or wider, within the bound.
A program may use at most 384 MiB of HBM per device.

v0:
```python
import functools
import math

import jax
import jax.numpy as jnp
from jax import lax
from jax.experimental import pallas as pl
from jax.experimental.pallas import tpu as pltpu
from jax.sharding import PartitionSpec as P

sharpness = 40.0
epsilon = 1e-06
exponent = 0.25

TILE = 128
PAIR = 2 * TILE
SCALE = sharpness * math.log2(math.e)


def gram_dot(a, b):
    return lax.dot_general(a, b, (((1,), (1,)), ((), ())), preferred_element_type=jnp.float32)


def fold_rows(x):
    return jnp.sum(x.reshape(x.shape[0] // 8, 8, x.shape[1]), axis=0)


def main_kernel(
    n_cell, tiles, occ_hbm, cond_ref, nb_ref, cnt_ref, eff_ref, sums_ref,
    ext, gram_a, gram_b, irow, icol, crow, ccol, acc, xin, wl,
    load_sem, halo_send, halo_recv, cond_send, cond_recv, acc_send, acc_recv,
):
    rows = tiles * TILE
    pairs = tiles // 2 + 1
    last = pairs - 1
    ext_rows = rows + PAIR
    species = ext.shape[1]
    me = lax.axis_index("cell")
    first_tile = (lax.axis_index("grp") * n_cell + me) * tiles
    has_left = me > 0
    has_right = me < n_cell - 1
    left = {"cell": jnp.maximum(me - 1, 0)}
    right = {"cell": jnp.minimum(me + 1, n_cell - 1)}
    mesh_id = pl.DeviceIdType.MESH

    def load(k):
        lo, hi = max(k * PAIR, TILE), min((k + 1) * PAIR, ext_rows - TILE)
        return pltpu.make_async_copy(
            occ_hbm.at[pl.ds(lo - TILE, hi - lo)], ext.at[pl.ds(lo, hi - lo)], load_sem.at[k]
        )

    for k in list(range(1, last)) + [0, last]:
        load(k).start()

    for t in range(tiles):
        crow[t + 1] = jnp.broadcast_to(cond_ref[t : t + 1, :], (8, TILE))

    barrier = pltpu.get_barrier_semaphore()

    @pl.when(has_left)
    def _():
        pl.semaphore_signal(barrier, inc=1, device_id=left, device_id_type=mesh_id)

    @pl.when(has_right)
    def _():
        pl.semaphore_signal(barrier, inc=1, device_id=right, device_id_type=mesh_id)

    pl.semaphore_wait(barrier, has_left.astype(jnp.int32) + has_right.astype(jnp.int32))

    def remote(src, dst, send, recv, slot, target):
        return pltpu.make_async_remote_copy(
            src_ref=src, dst_ref=dst, send_sem=send.at[slot], recv_sem=recv.at[slot],
            device_id=target, device_id_type=mesh_id,
        )

    halo_r = remote(
        occ_hbm.at[pl.ds(rows - TILE, TILE)], ext.at[pl.ds(0, TILE)], halo_send, halo_recv, 0, right
    )
    halo_l = remote(
        occ_hbm.at[pl.ds(0, TILE)], ext.at[pl.ds(ext_rows - TILE, TILE)], halo_send, halo_recv, 1, left
    )
    cond_r = remote(crow.at[tiles], crow.at[0], cond_send, cond_recv, 0, right)
    cond_l = remote(crow.at[1], crow.at[tiles + 1], cond_send, cond_recv, 1, left)
    acc_r = remote(acc.at[tiles + 1], xin.at[0], acc_send, acc_recv, 0, right)
    acc_l = remote(acc.at[0], xin.at[1], acc_send, acc_recv, 1, left)

    @pl.when(has_right)
    def _():
        halo_r.start()
        cond_r.start()

    @pl.when(has_left)
    def _():
        halo_l.start()
        cond_l.start()

    @pl.when(jnp.logical_not(has_left))
    def _():
        ext[pl.ds(0, TILE), :] = jnp.zeros((TILE, species), ext.dtype)
        crow[0] = jnp.zeros((8, TILE), jnp.float32)
        xin[0] = jnp.zeros((16, TILE), jnp.float32)

    @pl.when(jnp.logical_not(has_right))
    def _():
        ext[pl.ds(ext_rows - TILE, TILE), :] = jnp.zeros((TILE, species), ext.dtype)
        crow[tiles + 1] = jnp.zeros((8, TILE), jnp.float32)
        xin[1] = jnp.zeros((16, TILE), jnp.float32)

    def column(row8):
        return jnp.transpose(jnp.broadcast_to(row8[0:1, :], (TILE, TILE)))

    for e in range(1, tiles + 1):
        ccol[e] = column(crow[e])

    def hit(t, offset):
        wanted = first_tile + t + offset
        found = jnp.int32(0)
        for s in range(nb_ref.shape[1]):
            same = jnp.logical_and(nb_ref[t, s] == wanted, s < cnt_ref[t])
            found = jnp.maximum(found, same.astype(jnp.int32))
        return found.astype(jnp.float32)

    eye = lax.broadcasted_iota(jnp.int32, (TILE, TILE), 0) == lax.broadcasted_iota(
        jnp.int32, (TILE, TILE), 1
    )

    def part(ref, base, i, j):
        return ref[base + i * TILE : base + (i + 1) * TILE, j * TILE : (j + 1) * TILE]

    def own_own(ref, base, k, near, guest=None):
        e = 2 * k
        tiles_g = [[part(ref, base, i, j) for j in range(2)] for i in range(2)]
        rows_inv = []
        cols_inv = []
        for i in range(2):
            diag = jnp.sum(jnp.where(eye, tiles_g[i][i], 0.0), axis=0, keepdims=True)
            inv = jnp.broadcast_to(lax.rsqrt(diag + epsilon), (TILE, TILE))
            col = jnp.transpose(inv) * SCALE
            irow[e + i] = inv[0:8]
            icol[e + i] = col
            rows_inv.append(inv[0:1])
            cols_inv.append(col)
        cc = [ccol[e], ccol[e + 1]]
        w = [[None, None], [None, None]]
        for i in range(2):
            for j in range(2):
                v = jnp.exp2(tiles_g[i][j] * cols_inv[i] * rows_inv[j])
                if i == j and i == guest:
                    w[i][j] = jnp.zeros_like(v)
                elif i == j:
                    w[i][j] = jnp.where(eye, 0.0, v)
                else:
                    w[i][j] = v if near is None else v * near
        for j in range(2):
            if near is None:
                numer, denom = w[j][j] * cc[j], w[j][j]
            else:
                numer, denom = w[0][j] * cc[0] + w[1][j] * cc[1], w[0][j] + w[1][j]
            acc[e + j, 0:8, :] = fold_rows(numer)
            acc[e + j, 8:16, :] = fold_rows(denom)

    def prev_own(ref, base, k, far0, near1, far1):
        e = 2 * k
        r0, r1 = irow[e, 0:1, :], irow[e + 1, 0:1, :]
        w00 = jnp.exp2(part(ref, base, 0, 0) * icol[e - 2] * r0) * far0
        w10 = jnp.exp2(part(ref, base, 1, 0) * icol[e - 1] * r0) * near1
        w11 = jnp.exp2(part(ref, base, 1, 1) * icol[e - 1] * r1) * far1
        cp0, cp1 = ccol[e - 2], ccol[e - 1]
        acc[e, 0:8, :] += fold_rows(w00 * cp0 + w10 * cp1)
        acc[e, 8:16, :] += fold_rows(w00 + w10)
        acc[e + 1, 0:8, :] += fold_rows(w11 * cp1)
        acc[e + 1, 8:16, :] += fold_rows(w11)
        c0, c1 = crow[e, 0:1, :], crow[e + 1, 0:1, :]
        acc[e - 2, 0:8, :] += fold_rows(jnp.transpose(w00 * c0))
        acc[e - 2, 8:16, :] += fold_rows(jnp.transpose(w00))
        acc[e - 1, 0:8, :] += fold_rows(jnp.transpose(w10 * c0 + w11 * c1))
        acc[e - 1, 8:16, :] += fold_rows(jnp.transpose(w10 + w11))

    def pair_rows(k, count=1):
        start = k * PAIR
        if not isinstance(k, int):
            start = pl.multiple_of(start, PAIR)
        return ext[pl.ds(start, count * PAIR), :]

    def block(k, ref):
        ref[...] = gram_dot(pair_rows(k - 1, 2), pair_rows(k))

    def block_post(k, ref):
        own_own(ref, PAIR, k, hit(2 * k - 1, 1))
        prev_own(ref, 0, k, hit(2 * k - 3, 2), hit(2 * k - 2, 1), hit(2 * k - 2, 2))

    def wait_load(k):
        start = pl.multiple_of(k * PAIR, PAIR)
        pltpu.make_async_copy(
            occ_hbm.at[pl.ds(start - TILE, PAIR)], ext.at[pl.ds(start, PAIR)], load_sem.at[k]
        ).wait()

    load(1).wait()
    gram_b[0:PAIR, :] = gram_dot(pair_rows(1), pair_rows(1))
    load(2).wait()
    block(2, gram_a)
    own_own(gram_b, 0, 1, hit(1, 1))

    def two(i, carry):
        k = 2 * i + 3
        wait_load(k)
        block(k, gram_b)
        block_post(k - 1, gram_a)
        wait_load(k + 1)
        block(k + 1, gram_a)
        block_post(k, gram_b)
        return carry

    steps = (last - 3) // 2
    lax.fori_loop(0, steps, two, 0)
    tail = 2 * steps + 3
    current = gram_a
    for k in range(tail, last):
        other = gram_b if current is gram_a else gram_a
        load(k).wait()
        block(k, other)
        block_post(k - 1, current)
        current = other

    load(0).wait()
    load(last).wait()
    other = gram_b if current is gram_a else gram_a

    @pl.when(has_left)
    def _():
        halo_r.wait_recv()
        cond_r.wait_recv()

    @pl.when(has_right)
    def _():
        halo_l.wait_recv()
        cond_l.wait_recv()

    ccol[0] = column(crow[0])
    ccol[tiles + 1] = column(crow[tiles + 1])
    other[0:PAIR, :] = gram_dot(pair_rows(0), pair_rows(0))
    other[PAIR:, :] = gram_dot(pair_rows(0), pair_rows(1))
    block_post(last - 1, current)
    block(last, current)
    own_own(other, 0, 0, hit(0, -1), 0)
    prev_own(other, PAIR, 1, hit(1, -2), hit(0, 1), hit(0, 2))
    own_own(current, PAIR, last, None, 1)
    prev_own(current, 0, last, hit(tiles - 3, 2), hit(tiles - 2, 1), hit(tiles - 2, 2))

    @pl.when(has_right)
    def _():
        acc_r.start()

    @pl.when(has_left)
    def _():
        acc_l.start()

    line = lax.broadcasted_iota(jnp.int32, (16, TILE), 0)

    def finish(t, extra):
        e = t + 1
        total = acc[e]
        if extra is not None:
            total = total + xin[extra]
        numer = jnp.sum(total[0:8], axis=0, keepdims=True)
        denom = jnp.sum(total[8:16], axis=0, keepdims=True)
        eff = crow[e, 0:1, :] * numer / denom
        eff_ref[t : t + 1, :] = eff
        both = jnp.where(line == 0, eff, jnp.where(line == 1, 1.0, 0.0))
        wl[:, t * TILE : (t + 1) * TILE] = both.astype(jnp.bfloat16)

    for t in range(1, tiles - 1):
        finish(t, None)

    step = 512 if species % 512 == 0 else TILE

    def inner(i, carry):
        cols = pl.ds(pl.multiple_of(i * step, step), step)
        got = jnp.dot(
            wl[:, TILE : rows - TILE], ext[PAIR : rows, cols], preferred_element_type=jnp.float32
        )
        sums_ref[:, cols] = got[0:8]
        return carry

    lax.fori_loop(0, species // step, inner, 0)

    @pl.when(has_left)
    def _():
        acc_r.wait_recv()

    @pl.when(has_right)
    def _():
        acc_l.wait_recv()

    finish(0, 0)
    finish(tiles - 1, 1)

    def outer(i, carry):
        cols = pl.ds(pl.multiple_of(i * step, step), step)
        got = jnp.dot(
            wl[:, 0:TILE], ext[TILE:PAIR, cols], preferred_element_type=jnp.float32
        ) + jnp.dot(
            wl[:, rows - TILE : rows], ext[rows : rows + TILE, cols],
            preferred_element_type=jnp.float32,
        )
        sums_ref[:, cols] += got[0:8]
        return carry

    lax.fori_loop(0, species // step, outer, 0)

    @pl.when(has_right)
    def _():
        halo_r.wait_send()
        cond_r.wait_send()
        acc_r.wait_send()

    @pl.when(has_left)
    def _():
        halo_l.wait_send()
        cond_l.wait_send()
        acc_l.wait_send()


def exchange_kernel(n_cell, devices, per, wide, sums_ref, out_ref, got, send_sem, recv_sem):
    me = lax.axis_index("grp") * n_cell + lax.axis_index("cell")
    mesh_id = pl.DeviceIdType.MESH

    def block_of(owner):
        return sums_ref.at[:, pl.ds(pl.multiple_of((owner * per) // wide * wide, wide), wide)]

    def peer(j):
        owner = lax.rem(me + j, devices)
        return owner, (owner // n_cell, lax.rem(owner, n_cell))

    def copy(j):
        owner, target = peer(j)
        return pltpu.make_async_remote_copy(
            src_ref=block_of(owner), dst_ref=got.at[j], send_sem=send_sem.at[j],
            recv_sem=recv_sem.at[j], device_id=target, device_id_type=mesh_id,
        )

    barrier = pltpu.get_barrier_semaphore()

    def greet(j, carry):
        pl.semaphore_signal(barrier, inc=1, device_id=peer(j)[1], device_id_type=mesh_id)
        return carry

    def send(j, carry):
        copy(j).start()
        return carry

    def finish(j, carry):
        copy(j).wait()
        return carry

    lax.fori_loop(1, devices, greet, 0)
    pl.semaphore_wait(barrier, devices - 1)
    lax.fori_loop(1, devices, send, 0)
    got[0] = block_of(me)[...]
    lax.fori_loop(1, devices, finish, 0)
    out_ref[...] = jnp.sum(got[...], axis=0)


def per_device(n_cell, occurrence, condition, neighbours, pair_count):
    tiles = pair_count.shape[0]
    rows, species = occurrence.shape
    cond = condition.astype(jnp.float32).reshape(tiles, TILE)
    vmem = pl.BlockSpec(memory_space=pltpu.VMEM)
    smem = pl.BlockSpec(memory_space=pltpu.SMEM)
    effective, sums = pl.pallas_call(
        functools.partial(main_kernel, n_cell, tiles),
        out_shape=(
            jax.ShapeDtypeStruct((tiles, TILE), jnp.float32),
            jax.ShapeDtypeStruct((8, species), jnp.float32),
        ),
        in_specs=[pl.BlockSpec(memory_space=pl.ANY), vmem, smem, smem],
        out_specs=(vmem, vmem),
        scratch_shapes=[
            pltpu.VMEM((rows + PAIR, species), jnp.bfloat16),
            pltpu.VMEM((2 * PAIR, PAIR), jnp.float32),
            pltpu.VMEM((2 * PAIR, PAIR), jnp.float32),
            pltpu.VMEM((tiles + 2, 8, TILE), jnp.float32),
            pltpu.VMEM((tiles + 2, TILE, TILE), jnp.float32),
            pltpu.VMEM((tiles + 2, 8, TILE), jnp.float32),
            pltpu.VMEM((tiles + 2, TILE, TILE), jnp.float32),
            pltpu.VMEM((tiles + 2, 16, TILE), jnp.float32),
            pltpu.VMEM((2, 16, TILE), jnp.float32),
            pltpu.VMEM((16, rows), jnp.bfloat16),
            pltpu.SemaphoreType.DMA((tiles // 2 + 1,)),
            pltpu.SemaphoreType.DMA((2,)),
            pltpu.SemaphoreType.DMA((2,)),
            pltpu.SemaphoreType.DMA((2,)),
            pltpu.SemaphoreType.DMA((2,)),
            pltpu.SemaphoreType.DMA((2,)),
            pltpu.SemaphoreType.DMA((2,)),
        ],
        compiler_params=pltpu.CompilerParams(
            collective_id=0, has_side_effects=True, vmem_limit_bytes=56 * 2**20
        ),
    )(occurrence, cond, neighbours, pair_count)
    devices = lax.axis_size(("grp", "cell"))
    per = species // devices
    wide = max(per, TILE)
    totals = pl.pallas_call(
        functools.partial(exchange_kernel, n_cell, devices, per, wide),
        out_shape=jax.ShapeDtypeStruct((8, wide), jnp.float32),
        in_specs=[vmem],
        out_specs=vmem,
        scratch_shapes=[
            pltpu.VMEM((devices, 8, wide), jnp.float32),
            pltpu.SemaphoreType.DMA((devices,)),
            pltpu.SemaphoreType.DMA((devices,)),
        ],
        compiler_params=pltpu.CompilerParams(collective_id=1, has_side_effects=True),
    )(sums)
    if per < wide:
        offset = lax.rem(lax.axis_index(("grp", "cell")) * per, wide)
        totals = lax.dynamic_slice_in_dim(totals, offset, per, axis=1)
    persistence = (totals[0] / totals[1]) ** exponent
    return effective.reshape(rows), persistence


def solution(mesh):
    return jax.shard_map(
        functools.partial(per_device, mesh.shape["cell"]),
        mesh=mesh,
        in_specs=(
            P(("grp", "cell"), None),
            P(("grp", "cell")),
            P(("grp", "cell"), None),
            P(("grp", "cell")),
        ),
        out_specs=(P(("grp", "cell")), P(("grp", "cell"))),
        check_vma=False,
    )
```

profile of v0, /device:TPU:0, one launch (start us, length us, event | category | flops | bytes accessed | tf_op | source)
XLA Modules:
  0.0 53.6 jit_solution(8630720883615467166)
XLA Ops:
  0.6 1.3 %bitcast_convert_fusion.cond_ref = f32[24,128]{1,0:T(8,128)} fusion(bf16[3072]{0:T(1024)(128)(2,1)} %param.5), kind=kLoop, calls=%fused_computation | loop fusion | flops 3072 | bytes 18432 | tf_op jit(solution)/shard_map/reshape | solution.py:367
  1.9 1.4 %copy.6.nb_ref = s32[24,4]{1,0:T(8,128)} copy(s32[24,4]{0,1:T(4,128)} %param.6) | data formatting | bytes 768 | tf_op args[2]
  3.3 34.5 %shard_map.59 = (f32[24,128]{1,0:T(8,128)}, f32[8,4096]{1,0:T(8,128)}) custom-call(bf16[3072,4096]{1,0:T(8,128)(2,1)} %occ_hbm.1, f32[24,128]{1,0:T(8,128)} %bitcast_convert_fusion.cond_ref, s32[24,4]{1,0:T(8,128)} %copy.6.nb_ref, s32[24]{0:T(128)} %cnt_ref.1), custom_call_target="tpu_custom_call" | custom-call | tf_op jit(solution)/shard_map/pallas_call | solution.py:370
  37.7 13.3 %shard_map.60 = f32[8,128]{1,0:T(8,128)} custom-call(f32[8,4096]{1,0:T(8,128)} %get-tuple-element.5.sums_ref), custom_call_target="tpu_custom_call" | custom-call | tf_op jit(solution)/shard_map/pallas_call | solution.py:404
  51.1 1.3 %power_bitcast_fusion = f32[128]{0:T(128)} fusion(f32[8,128]{1,0:T(8,128)} %shard_map.60), kind=kLoop, calls=%fused_computation.1 | loop fusion | flops 128 | bytes 1536 | tf_op jit(solution)/shard_map/pow | solution.py:419
  52.3 1.3 %copy.8 = f32[3072]{0:T(1024)} copy(f32[3072]{0:T(1024)} %bitcast.6) | data formatting | bytes 24576
where the time goes:
time: 54.1 us; the launch traced here: 53.6 us
  Pallas kernels  47.8 us (88%)
  local copies, waits for them, and re-layouts  2.66 us (5%)
  other arithmetic  2.57 us (5%)
  between operations  0.65 us (1%)
    pallas_call x1, Pallas kernels, per_device(): pl.pallas_call(functools.partial(main_kernel, n_cell, tiles), out_shape=(...  34.5 us
    pallas_call x1, Pallas kernels, per_device(): pl.pallas_call(functools.partial(exchange_kernel, n_cell, devices, per, w...  13.3 us
    unnamed x2, local copies, waits for them, and re-layouts  2.66 us
    reshape x1, other arithmetic, per_device(): cond = condition.astype(jnp.float32).reshape(tiles, TILE)  1.29 us
    pow x1, other arithmetic, per_device(): persistence = (totals[0] / totals[1]) ** exponent  1.28 us

commit v1 on v0

v1 whole, which is shorter than its diff:
```python
import functools
import math

import jax
import jax.numpy as jnp
from jax import lax
from jax.experimental import pallas as pl
from jax.experimental.pallas import tpu as pltpu
from jax.sharding import PartitionSpec as P

sharpness = 40.0
epsilon = 1e-06

TILE = 128
PAIR = 2 * TILE
SCALE = sharpness * math.log2(math.e)


def gram_dot(a, b):
    return lax.dot_general(a, b, (((1,), (1,)), ((), ())), preferred_element_type=jnp.float32)


def fold_rows(x):
    return jnp.sum(x.reshape(x.shape[0] // 8, 8, x.shape[1]), axis=0)


def doubling(reach):
    steps = []
    d = 1
    while d < reach:
        steps.append(d)
        d *= 2
    return steps


def main_kernel(
    n_grp, n_cell, tiles, per, wide, occ_hbm, cond_ref, nb_ref, cnt_ref, eff_ref, tot_ref,
    own, halo, gram, irow, icol, crow, ccol, acc, xin, wl, sums, got,
    load_sem, halo_send, halo_recv, cond_send, cond_recv, acc_send, acc_recv,
    sum_send, sum_recv, from_left, from_right, from_before, from_after,
):
    rows = tiles * TILE
    pairs = tiles // 2
    species = own.shape[1]
    devices = n_grp * n_cell
    grp = lax.axis_index("grp")
    me = lax.axis_index("cell")
    rank = grp * n_cell + me
    first_tile = rank * tiles
    has_left = me > 0
    has_right = me < n_cell - 1
    left = (grp, jnp.maximum(me - 1, 0))
    right = (grp, jnp.minimum(me + 1, n_cell - 1))
    mesh_id = pl.DeviceIdType.MESH

    def load(k):
        start = k * PAIR if isinstance(k, int) else pl.multiple_of(k * PAIR, PAIR)
        return pltpu.make_async_copy(
            occ_hbm.at[pl.ds(start, PAIR)], own.at[pl.ds(start, PAIR)], load_sem.at[k]
        )

    barrier = pltpu.get_barrier_semaphore()

    @pl.when(has_left)
    def _():
        pl.semaphore_signal(barrier, inc=1, device_id=left, device_id_type=mesh_id)

    @pl.when(has_right)
    def _():
        pl.semaphore_signal(barrier, inc=1, device_id=right, device_id_type=mesh_id)

    for shift in (1, n_grp - 1):
        pl.semaphore_signal(
            barrier, inc=1, device_id=(lax.rem(grp + shift, n_grp), me), device_id_type=mesh_id
        )

    for k in range(pairs):
        load(k).start()

    cond = cond_ref[...].astype(jnp.float32)
    for t in range(tiles):
        crow[t + 1] = jnp.broadcast_to(cond[t : t + 1, :], (8, TILE))

    pl.semaphore_wait(barrier, has_left.astype(jnp.int32) + has_right.astype(jnp.int32) + 2)

    def remote(src, dst, send, recv, slot, target):
        return pltpu.make_async_remote_copy(
            src_ref=src, dst_ref=dst, send_sem=send.at[slot], recv_sem=recv.at[slot],
            device_id=target, device_id_type=mesh_id,
        )

    halo_r = remote(
        occ_hbm.at[pl.ds(rows - TILE, TILE)], halo.at[0], halo_send, halo_recv, 0, right
    )
    halo_l = remote(occ_hbm.at[pl.ds(0, TILE)], halo.at[1], halo_send, halo_recv, 1, left)
    cond_r = remote(crow.at[tiles], crow.at[0], cond_send, cond_recv, 0, right)
    cond_l = remote(crow.at[1], crow.at[tiles + 1], cond_send, cond_recv, 1, left)
    acc_r = remote(acc.at[tiles + 1], xin.at[0], acc_send, acc_recv, 0, right)
    acc_l = remote(acc.at[0], xin.at[1], acc_send, acc_recv, 1, left)

    @pl.when(has_right)
    def _():
        halo_r.start()
        cond_r.start()

    @pl.when(has_left)
    def _():
        halo_l.start()
        cond_l.start()

    @pl.when(jnp.logical_not(has_left))
    def _():
        halo[0] = jnp.zeros((TILE, species), halo.dtype)
        crow[0] = jnp.zeros((8, TILE), jnp.float32)
        xin[0] = jnp.zeros((16, TILE), jnp.float32)

    @pl.when(jnp.logical_not(has_right))
    def _():
        halo[1] = jnp.zeros((TILE, species), halo.dtype)
        crow[tiles + 1] = jnp.zeros((8, TILE), jnp.float32)
        xin[1] = jnp.zeros((16, TILE), jnp.float32)

    def grp_round(r, d):
        for shift, sem in ((d, from_before), (n_grp - d, from_after)):
            pl.semaphore_signal(
                sem.at[r], inc=1, device_id=(lax.rem(grp + shift, n_grp), me), device_id_type=mesh_id
            )
        pl.semaphore_wait(from_before.at[r], 1)
        pl.semaphore_wait(from_after.at[r], 1)

    def cell_round(r, d):
        low = me >= d
        high = me + d < n_cell

        @pl.when(low)
        def _():
            pl.semaphore_signal(
                from_right.at[r], inc=1, device_id=(grp, jnp.maximum(me - d, 0)),
                device_id_type=mesh_id,
            )

        @pl.when(high)
        def _():
            pl.semaphore_signal(
                from_left.at[r], inc=1, device_id=(grp, jnp.minimum(me + d, n_cell - 1)),
                device_id_type=mesh_id,
            )

        @pl.when(low)
        def _():
            pl.semaphore_wait(from_left.at[r], 1)

        @pl.when(high)
        def _():
            pl.semaphore_wait(from_right.at[r], 1)

    rounds = [
        functools.partial(grp_round, r, d) for r, d in enumerate(doubling((n_grp + 1) // 2))
    ]
    rounds += [functools.partial(cell_round, r, d) for r, d in enumerate(doubling(n_cell))]

    def column(row8):
        return jnp.transpose(jnp.broadcast_to(row8[0:1, :], (TILE, TILE)))

    for e in range(1, tiles + 1):
        ccol[e] = column(crow[e])

    def hit(t, offset):
        wanted = first_tile + t + offset
        found = jnp.int32(0)
        for s in range(nb_ref.shape[0]):
            same = jnp.logical_and(nb_ref[s, t] == wanted, s < cnt_ref[t])
            found = jnp.maximum(found, same.astype(jnp.int32))
        return found.astype(jnp.float32)

    eye = lax.broadcasted_iota(jnp.int32, (TILE, TILE), 0) == lax.broadcasted_iota(
        jnp.int32, (TILE, TILE), 1
    )

    def part(slot, base, i, j):
        return gram[slot, base + i * TILE : base + (i + 1) * TILE, j * TILE : (j + 1) * TILE]

    def own_own(slot, base, k):
        e = 2 * k + 1
        near = hit(2 * k, 1)
        tiles_g = [[part(slot, base, i, j) for j in range(2)] for i in range(2)]
        rows_inv = []
        cols_inv = []
        for i in range(2):
            diag = jnp.sum(jnp.where(eye, tiles_g[i][i], 0.0), axis=0, keepdims=True)
            inv = jnp.broadcast_to(lax.rsqrt(diag + epsilon), (TILE, TILE))
            col = jnp.transpose(inv) * SCALE
            irow[e + i] = inv[0:8]
            icol[e + i] = col
            rows_inv.append(inv[0:1])
            cols_inv.append(col)
        cc = [ccol[e], ccol[e + 1]]
        w = [[None, None], [None, None]]
        for i in range(2):
            for j in range(2):
                v = jnp.exp2(tiles_g[i][j] * cols_inv[i] * rows_inv[j])
                w[i][j] = jnp.where(eye, 0.0, v) if i == j else v * near
        for j in range(2):
            acc[e + j, 0:8, :] = fold_rows(w[0][j] * cc[0] + w[1][j] * cc[1])
            acc[e + j, 8:16, :] = fold_rows(w[0][j] + w[1][j])

    def prev_own(slot, k):
        e = 2 * k + 1
        far0, near1, far1 = hit(2 * k - 2, 2), hit(2 * k - 1, 1), hit(2 * k - 1, 2)
        r0, r1 = irow[e, 0:1, :], irow[e + 1, 0:1, :]
        w00 = jnp.exp2(part(slot, 0, 0, 0) * icol[e - 2] * r0) * far0
        w10 = jnp.exp2(part(slot, 0, 1, 0) * icol[e - 1] * r0) * near1
        w11 = jnp.exp2(part(slot, 0, 1, 1) * icol[e - 1] * r1) * far1
        cp0, cp1 = ccol[e - 2], ccol[e - 1]
        acc[e, 0:8, :] += fold_rows(w00 * cp0 + w10 * cp1)
        acc[e, 8:16, :] += fold_rows(w00 + w10)
        acc[e + 1, 0:8, :] += fold_rows(w11 * cp1)
        acc[e + 1, 8:16, :] += fold_rows(w11)
        c0, c1 = crow[e, 0:1, :], crow[e + 1, 0:1, :]
        acc[e - 2, 0:8, :] += fold_rows(jnp.transpose(w00 * c0))
        acc[e - 2, 8:16, :] += fold_rows(jnp.transpose(w00))
        acc[e - 1, 0:8, :] += fold_rows(jnp.transpose(w10 * c0 + w11 * c1))
        acc[e - 1, 8:16, :] += fold_rows(jnp.transpose(w10 + w11))

    def pair_rows(k, count=1):
        start = k * PAIR if isinstance(k, int) else pl.multiple_of(k * PAIR, PAIR)
        return own[pl.ds(start, count * PAIR), :]

    def block(k, slot):
        gram[slot] = gram_dot(pair_rows(k - 1, 2), pair_rows(k))

    load(0).wait()
    gram[0, PAIR:, :] = gram_dot(pair_rows(0), pair_rows(0))
    load(1).wait()
    block(1, 1)
    own_own(0, PAIR, 0)

    def step(i, carry):
        k = i + 2
        slot = lax.rem(k, 2)
        load(k).wait()
        block(k, slot)
        own_own(1 - slot, PAIR, k - 1)
        prev_own(1 - slot, k - 1)
        for r, one in enumerate(rounds):
            pl.when(i == min(r + 1, pairs - 3))(one)
        return carry

    lax.fori_loop(0, pairs - 2, step, 0)
    slot = (pairs - 1) % 2
    own_own(slot, PAIR, pairs - 1)
    prev_own(slot, pairs - 1)

    @pl.when(has_left)
    def _():
        halo_r.wait_recv()
        cond_r.wait_recv()

    @pl.when(has_right)
    def _():
        halo_l.wait_recv()
        cond_l.wait_recv()

    ccol[0] = column(crow[0])
    ccol[tiles + 1] = column(crow[tiles + 1])

    def halo_inverse(side):
        total = jnp.zeros((TILE, TILE), jnp.float32)
        for q in range(species // TILE):
            x = halo[side, :, q * TILE : (q + 1) * TILE].astype(jnp.float32)
            total = total + x * x
        return lax.rsqrt(jnp.sum(total, axis=1, keepdims=True) + epsilon) * SCALE

    edge_l = gram_dot(halo[0], pair_rows(0))
    edge_r = gram_dot(halo[1], own[rows - PAIR : rows - TILE, :])
    inv_l = jnp.broadcast_to(halo_inverse(0), (TILE, TILE))
    inv_r = jnp.broadcast_to(halo_inverse(1), (TILE, TILE))
    w0 = jnp.exp2(edge_l[:, 0:TILE] * inv_l * irow[1, 0:1, :]) * hit(0, -1)
    w1 = jnp.exp2(edge_l[:, TILE:] * inv_l * irow[2, 0:1, :]) * hit(1, -2)
    acc[0, 0:8, :] = fold_rows(jnp.transpose(w0 * crow[1, 0:1, :] + w1 * crow[2, 0:1, :]))
    acc[0, 8:16, :] = fold_rows(jnp.transpose(w0 + w1))
    w2 = jnp.exp2(edge_r * inv_r * irow[tiles - 1, 0:1, :]) * hit(tiles - 2, 2)
    acc[tiles + 1, 0:8, :] = fold_rows(jnp.transpose(w2 * crow[tiles - 1, 0:1, :]))
    acc[tiles + 1, 8:16, :] = fold_rows(jnp.transpose(w2))

    @pl.when(has_right)
    def _():
        acc_r.start()

    @pl.when(has_left)
    def _():
        acc_l.start()

    acc[1, 0:8, :] += fold_rows(w0 * ccol[0])
    acc[1, 8:16, :] += fold_rows(w0)
    acc[2, 0:8, :] += fold_rows(w1 * ccol[0])
    acc[2, 8:16, :] += fold_rows(w1)
    acc[tiles - 1, 0:8, :] += fold_rows(w2 * ccol[tiles + 1])
    acc[tiles - 1, 8:16, :] += fold_rows(w2)

    line = lax.broadcasted_iota(jnp.int32, (16, TILE), 0)

    def finish(t, extra=None):
        e = t + 1
        total = acc[e]
        if extra is not None:
            total = total + xin[extra]
        numer = jnp.sum(total[0:8], axis=0, keepdims=True)
        denom = jnp.sum(total[8:16], axis=0, keepdims=True)
        eff = crow[e, 0:1, :] * numer / denom
        eff_ref[t : t + 1, :] = eff
        both = jnp.where(line == 0, eff, jnp.where(line == 1, 1.0, 0.0))
        wl[:, t * TILE : (t + 1) * TILE] = both.astype(jnp.bfloat16)

    for t in range(1, tiles - 1):
        finish(t)

    wide_step = 512 if species % 512 == 0 else TILE
    blocks = wide_step // TILE

    def inner(i, carry):
        cols = pl.ds(pl.multiple_of(i * wide_step, wide_step), wide_step)
        value = jnp.dot(
            wl[:, PAIR : rows - PAIR], own[PAIR : rows - PAIR, cols],
            preferred_element_type=jnp.float32,
        )
        for q in range(blocks):
            sums[i * blocks + q] = value[0:2, q * TILE : (q + 1) * TILE]
        return carry

    lax.fori_loop(0, species // wide_step, inner, 0)

    @pl.when(has_left)
    def _():
        acc_r.wait_recv()

    @pl.when(has_right)
    def _():
        acc_l.wait_recv()

    finish(0, 0)
    finish(tiles - 1, 1)

    def outer(i, carry):
        cols = pl.ds(pl.multiple_of(i * wide_step, wide_step), wide_step)
        value = jnp.dot(
            wl[:, 0:PAIR], own[0:PAIR, cols], preferred_element_type=jnp.float32
        ) + jnp.dot(
            wl[:, rows - PAIR : rows], own[rows - PAIR : rows, cols],
            preferred_element_type=jnp.float32,
        )
        for q in range(blocks):
            sums[i * blocks + q] += value[0:2, q * TILE : (q + 1) * TILE]
        return carry

    lax.fori_loop(0, species // wide_step, outer, 0)

    def send(j, carry):
        owner = lax.rem(rank + j, devices)
        pltpu.make_async_remote_copy(
            src_ref=sums.at[owner * per // wide], dst_ref=got.at[j], send_sem=sum_send,
            recv_sem=sum_recv, device_id=(owner // n_cell, lax.rem(owner, n_cell)),
            device_id_type=mesh_id,
        ).start()
        return carry

    lax.fori_loop(1, devices, send, 0)
    got[0] = sums[rank * per // wide]
    others = got.at[pl.ds(1, devices - 1)]
    pltpu.make_async_copy(others, others, sum_recv).wait()
    tot_ref[...] = jnp.sum(got[...], axis=0)
    pltpu.make_async_copy(others, others, sum_send).wait()

    @pl.when(has_right)
    def _():
        halo_r.wait_send()
        cond_r.wait_send()
        acc_r.wait_send()

    @pl.when(has_left)
    def _():
        halo_l.wait_send()
        cond_l.wait_send()
        acc_l.wait_send()


def close_kernel(eff_ref, tot_ref, eff_out, per_out):
    eff_out[...] = eff_ref[...]
    per_out[...] = jnp.sqrt(jnp.sqrt(tot_ref[0:1, :] / tot_ref[1:2, :]))


def per_device(n_grp, n_cell, occurrence, condition, neighbours, pair_count):
    tiles = pair_count.shape[0]
    rows, species = occurrence.shape
    devices = n_grp * n_cell
    per = species // devices
    wide = max(per, TILE)
    vmem = pl.BlockSpec(memory_space=pltpu.VMEM)
    smem = pl.BlockSpec(memory_space=pltpu.SMEM)
    dma = pltpu.SemaphoreType.DMA
    cell_sems = pltpu.SemaphoreType.REGULAR((max(len(doubling(n_cell)), 1),))
    grp_sems = pltpu.SemaphoreType.REGULAR((max(len(doubling((n_grp + 1) // 2)), 1),))
    effective, totals = pl.pallas_call(
        functools.partial(main_kernel, n_grp, n_cell, tiles, per, wide),
        out_shape=(
            jax.ShapeDtypeStruct((tiles, TILE), jnp.float32),
            jax.ShapeDtypeStruct((2, wide), jnp.float32),
        ),
        in_specs=[pl.BlockSpec(memory_space=pl.ANY), vmem, smem, smem],
        out_specs=(vmem, vmem),
        scratch_shapes=[
            pltpu.VMEM((rows, species), jnp.bfloat16),
            pltpu.VMEM((2, TILE, species), jnp.bfloat16),
            pltpu.VMEM((2, 2 * PAIR, PAIR), jnp.float32),
            pltpu.VMEM((tiles + 2, 8, TILE), jnp.float32),
            pltpu.VMEM((tiles + 2, TILE, TILE), jnp.float32),
            pltpu.VMEM((tiles + 2, 8, TILE), jnp.float32),
            pltpu.VMEM((tiles + 2, TILE, TILE), jnp.float32),
            pltpu.VMEM((tiles + 2, 16, TILE), jnp.float32),
            pltpu.VMEM((2, 16, TILE), jnp.float32),
            pltpu.VMEM((16, rows), jnp.bfloat16),
            pltpu.VMEM((species // wide, 2, wide), jnp.float32),
            pltpu.VMEM((devices, 2, wide), jnp.float32),
            dma((tiles // 2,)), dma((2,)), dma((2,)), dma((2,)), dma((2,)), dma((2,)), dma((2,)),
            dma, dma, cell_sems, cell_sems, grp_sems, grp_sems,
        ],
        compiler_params=pltpu.CompilerParams(
            collective_id=0, has_side_effects=True, vmem_limit_bytes=56 * 2**20
        ),
    )(occurrence, condition.reshape(tiles, TILE), neighbours.T, pair_count)
    effective, persistence = pl.pallas_call(
        close_kernel,
        out_shape=(
            jax.ShapeDtypeStruct((tiles, TILE), jnp.float32),
            jax.ShapeDtypeStruct((1, wide), jnp.float32),
        ),
        in_specs=[vmem, vmem],
        out_specs=(vmem, vmem),
    )(effective, totals)
    persistence = persistence.reshape(wide)
    if per < wide:
        offset = lax.rem(lax.axis_index(("grp", "cell")) * per, wide)
        persistence = lax.dynamic_slice_in_dim(persistence, offset, per)
    return effective.reshape(rows), persistence


def solution(mesh):
    return jax.shard_map(
        functools.partial(per_device, mesh.shape["grp"], mesh.shape["cell"]),
        mesh=mesh,
        in_specs=(
            P(("grp", "cell"), None),
            P(("grp", "cell")),
            P(("grp", "cell"), None),
            P(("grp", "cell")),
        ),
        out_specs=(P(("grp", "cell")), P(("grp", "cell"))),
        check_vma=False,
    )
```

time: 54.1 us -> 43.4 us (0.80)
  Pallas kernels: 47.8 us -> 42.5 us
  local copies, waits for them, and re-layouts: 2.66 us -> 0 us
  other arithmetic: 2.57 us -> 0 us
    pallas_call x2, Pallas kernels: 47.8 us -> 42.5 us  [the longest x1 41.1 us: per_device(): pl.pallas_call(functools.partial(main_kernel, n_grp, n_cell, tiles, per,...]
    unnamed x2 -> x0, local copies, waits for them, and re-layouts: 2.66 us -> none
    reshape x1 -> x0, other arithmetic: 1.29 us -> none  [per_device(): cond = condition.astype(jnp.float32).reshape(tiles, TILE)]
    pow x1 -> x0, other arithmetic: 1.28 us -> none  [per_device(): persistence = (totals[0] / totals[1]) ** exponent]
where the time goes in v1:
time: 43.4 us; the launch traced here: 43.1 us
  Pallas kernels  42.5 us (98%)
  between operations  0.64 us (1%)
    pallas_call x1, Pallas kernels, per_device(): pl.pallas_call(functools.partial(main_kernel, n_grp, n_cell, tiles, per,...  41.1 us
    pallas_call x1, Pallas kernels, per_device(): pl.pallas_call(close_kernel, out_shape=(jax.ShapeDtypeStruct((tiles, TILE...  1.31 us

profile of v1, /device:TPU:0, one launch (start us, length us, event | category | flops | bytes accessed | tf_op | source)
XLA Modules:
  0.0 43.1 jit_solution(3195219637615600781)
XLA Ops:
  0.6 41.1 %shard_map.59 = (f32[24,128]{1,0:T(8,128)}, f32[2,128]{1,0:T(2,128)}) custom-call(bf16[3072,4096]{1,0:T(8,128)(2,1)} %occ_hbm.1, bf16[24,128]{1,0:T(8,128)(2,1)} %bitcast.4, s32[4,24]{1,0:T(4,128)} %bitcast.5, s32[24]{0:T(128)} %cnt_ref.1), custom_call_target="tpu_custom_call" | custom-call | tf_op jit(solution)/shard_map/pallas_call | solution.py:403
  41.8 1.3 %shard_map.60 = (f32[24,128]{1,0:T(8,128)}, f32[1,128]{1,0:T(1,128)}) custom-call(f32[24,128]{1,0:T(8,128)} %get-tuple-element.6.eff_ref, f32[2,128]{1,0:T(2,128)} %get-tuple-element.7.tot_ref), custom_call_target="tpu_custom_call" | custom-call | tf_op jit(solution)/shard_map/pallas_call | solution.py:431

commit v2 on v1

--- a/solution.py
+++ b/solution.py
@@ -13,6 +13,7 @@
 
 TILE = 128
 PAIR = 2 * TILE
+GROUP = 2
 SCALE = sharpness * math.log2(math.e)
 
 
@@ -22,22 +23,13 @@
 
 def fold_rows(x):
     return jnp.sum(x.reshape(x.shape[0] // 8, 8, x.shape[1]), axis=0)
-
-
-def doubling(reach):
-    steps = []
-    d = 1
-    while d < reach:
-        steps.append(d)
-        d *= 2
-    return steps
 
 
 def main_kernel(
     n_grp, n_cell, tiles, per, wide, occ_hbm, cond_ref, nb_ref, cnt_ref, eff_ref, tot_ref,
     own, halo, gram, irow, icol, crow, ccol, acc, xin, wl, sums, got,
     load_sem, halo_send, halo_recv, cond_send, cond_recv, acc_send, acc_recv,
-    sum_send, sum_recv, from_left, from_right, from_before, from_after,
+    sum_send, sum_recv,
 ):
     rows = tiles * TILE
     pairs = tiles // 2
@@ -61,27 +53,25 @@
 
     barrier = pltpu.get_barrier_semaphore()
 
-    @pl.when(has_left)
-    def _():
-        pl.semaphore_signal(barrier, inc=1, device_id=left, device_id_type=mesh_id)
-
-    @pl.when(has_right)
-    def _():
-        pl.semaphore_signal(barrier, inc=1, device_id=right, device_id_type=mesh_id)
-
-    for shift in (1, n_grp - 1):
+    for k in range(2):
+        load(k).start()
+
+    def greet(j, carry):
+        other = lax.rem(rank + j, devices)
         pl.semaphore_signal(
-            barrier, inc=1, device_id=(lax.rem(grp + shift, n_grp), me), device_id_type=mesh_id
+            barrier, inc=1, device_id=(other // n_cell, lax.rem(other, n_cell)),
+            device_id_type=mesh_id,
         )
-
-    for k in range(pairs):
+        return carry
+
+    lax.fori_loop(1, devices, greet, 0, unroll=True)
+
+    for k in range(2, pairs):
         load(k).start()
 
     cond = cond_ref[...].astype(jnp.float32)
     for t in range(tiles):
         crow[t + 1] = jnp.broadcast_to(cond[t : t + 1, :], (8, TILE))
-
-    pl.semaphore_wait(barrier, has_left.astype(jnp.int32) + has_right.astype(jnp.int32) + 2)
 
     def remote(src, dst, send, recv, slot, target):
         return pltpu.make_async_remote_copy(
@@ -98,72 +88,8 @@
     acc_r = remote(acc.at[tiles + 1], xin.at[0], acc_send, acc_recv, 0, right)
     acc_l = remote(acc.at[0], xin.at[1], acc_send, acc_recv, 1, left)
 
-    @pl.when(has_right)
-    def _():
-        halo_r.start()
-        cond_r.start()
-
-    @pl.when(has_left)
-    def _():
-        halo_l.start()
-        cond_l.start()
-
-    @pl.when(jnp.logical_not(has_left))
-    def _():
-        halo[0] = jnp.zeros((TILE, species), halo.dtype)
-        crow[0] = jnp.zeros((8, TILE), jnp.float32)
-        xin[0] = jnp.zeros((16, TILE), jnp.float32)
-
-    @pl.when(jnp.logical_not(has_right))
-    def _():
-        halo[1] = jnp.zeros((TILE, species), halo.dtype)
-        crow[tiles + 1] = jnp.zeros((8, TILE), jnp.float32)
-        xin[1] = jnp.zeros((16, TILE), jnp.float32)
-
-    def grp_round(r, d):
-        for shift, sem in ((d, from_before), (n_grp - d, from_after)):
-            pl.semaphore_signal(
-                sem.at[r], inc=1, device_id=(lax.rem(grp + shift, n_grp), me), device_id_type=mesh_id
-            )
-        pl.semaphore_wait(from_before.at[r], 1)
-        pl.semaphore_wait(from_after.at[r], 1)
-
-    def cell_round(r, d):
-        low = me >= d
-        high = me + d < n_cell
-
-        @pl.when(low)
-        def _():
-            pl.semaphore_signal(
-                from_right.at[r], inc=1, device_id=(grp, jnp.maximum(me - d, 0)),
-                device_id_type=mesh_id,
-            )
-
-        @pl.when(high)
-        def _():
-            pl.semaphore_signal(
-                from_left.at[r], inc=1, device_id=(grp, jnp.minimum(me + d, n_cell - 1)),
-                device_id_type=mesh_id,
-            )
-
-        @pl.when(low)
-        def _():
-            pl.semaphore_wait(from_left.at[r], 1)
-
-        @pl.when(high)
-        def _():
-            pl.semaphore_wait(from_right.at[r], 1)
-
-    rounds = [
-        functools.partial(grp_round, r, d) for r, d in enumerate(doubling((n_grp + 1) // 2))
-    ]
-    rounds += [functools.partial(cell_round, r, d) for r, d in enumerate(doubling(n_cell))]
-
     def column(row8):
         return jnp.transpose(jnp.broadcast_to(row8[0:1, :], (TILE, TILE)))
-
-    for e in range(1, tiles + 1):
-        ccol[e] = column(crow[e])
 
     def hit(t, offset):
         wanted = first_tile + t + offset
@@ -194,7 +120,9 @@
             icol[e + i] = col
             rows_inv.append(inv[0:1])
             cols_inv.append(col)
-        cc = [ccol[e], ccol[e + 1]]
+        cc = [column(crow[e]), column(crow[e + 1])]
+        ccol[e] = cc[0]
+        ccol[e + 1] = cc[1]
         w = [[None, None], [None, None]]
         for i in range(2):
             for j in range(2):
@@ -231,22 +159,51 @@
 
     load(0).wait()
     gram[0, PAIR:, :] = gram_dot(pair_rows(0), pair_rows(0))
+    pl.semaphore_wait(barrier, devices - 1)
+
+    @pl.when(has_right)
+    def _():
+        halo_r.start()
+        cond_r.start()
+
+    @pl.when(has_left)
+    def _():
+        halo_l.start()
+        cond_l.start()
+
+    @pl.when(jnp.logical_not(has_left))
+    def _():
+        halo[0] = jnp.zeros((TILE, species), halo.dtype)
+        crow[0] = jnp.zeros((8, TILE), jnp.float32)
+        xin[0] = jnp.zeros((16, TILE), jnp.float32)
+
+    @pl.when(jnp.logical_not(has_right))
+    def _():
+        halo[1] = jnp.zeros((TILE, species), halo.dtype)
+        crow[tiles + 1] = jnp.zeros((8, TILE), jnp.float32)
+        xin[1] = jnp.zeros((16, TILE), jnp.float32)
+
     load(1).wait()
     block(1, 1)
     own_own(0, PAIR, 0)
 
     def step(i, carry):
-        k = i + 2
-        slot = lax.rem(k, 2)
+        first = 2 + GROUP * i
+        for u in range(GROUP):
+            load(first + u).wait()
+        for u in range(GROUP):
+            block(first + u, u % 2)
+            own_own(1 - u % 2, PAIR, first + u - 1)
+            prev_own(1 - u % 2, first + u - 1)
+        return carry
+
+    steps = (pairs - 2) // GROUP
+    lax.fori_loop(0, steps, step, 0)
+    for k in range(2 + GROUP * steps, pairs):
         load(k).wait()
-        block(k, slot)
-        own_own(1 - slot, PAIR, k - 1)
-        prev_own(1 - slot, k - 1)
-        for r, one in enumerate(rounds):
-            pl.when(i == min(r + 1, pairs - 3))(one)
-        return carry
-
-    lax.fori_loop(0, pairs - 2, step, 0)
+        block(k, k % 2)
+        own_own(1 - k % 2, PAIR, k - 1)
+        prev_own(1 - k % 2, k - 1)
     slot = (pairs - 1) % 2
     own_own(slot, PAIR, pairs - 1)
     prev_own(slot, pairs - 1)
@@ -341,8 +298,11 @@
     finish(0, 0)
     finish(tiles - 1, 1)
 
+    share = wide // per
+
     def outer(i, carry):
-        cols = pl.ds(pl.multiple_of(i * wide_step, wide_step), wide_step)
+        chunk = lax.rem(i + rank // (blocks * share), species // wide_step)
+        cols = pl.ds(pl.multiple_of(chunk * wide_step, wide_step), wide_step)
         value = jnp.dot(
             wl[:, 0:PAIR], own[0:PAIR, cols], preferred_element_type=jnp.float32
         ) + jnp.dot(
@@ -350,22 +310,23 @@
             preferred_element_type=jnp.float32,
         )
         for q in range(blocks):
-            sums[i * blocks + q] += value[0:2, q * TILE : (q + 1) * TILE]
+            sums[chunk * blocks + q] += value[0:2, q * TILE : (q + 1) * TILE]
+        for q in range(blocks * share):
+            owner = chunk * blocks * share + q
+
+            @pl.when(owner != rank)
+            def _():
+                pltpu.make_async_remote_copy(
+                    src_ref=sums.at[chunk * blocks + q // share],
+                    dst_ref=got.at[lax.rem(rank - owner + devices, devices)],
+                    send_sem=sum_send, recv_sem=sum_recv,
+                    device_id=(owner // n_cell, lax.rem(owner, n_cell)), device_id_type=mesh_id,
+                ).start()
+
         return carry
 
     lax.fori_loop(0, species // wide_step, outer, 0)
-
-    def send(j, carry):
-        owner = lax.rem(rank + j, devices)
-        pltpu.make_async_remote_copy(
-            src_ref=sums.at[owner * per // wide], dst_ref=got.at[j], send_sem=sum_send,
-            recv_sem=sum_recv, device_id=(owner // n_cell, lax.rem(owner, n_cell)),
-            device_id_type=mesh_id,
-        ).start()
-        return carry
-
-    lax.fori_loop(1, devices, send, 0)
-    got[0] = sums[rank * per // wide]
+    got[0] = sums[rank // share]
     others = got.at[pl.ds(1, devices - 1)]
     pltpu.make_async_copy(others, others, sum_recv).wait()
     tot_ref[...] = jnp.sum(got[...], axis=0)
@@ -398,8 +359,6 @@
     vmem = pl.BlockSpec(memory_space=pltpu.VMEM)
     smem = pl.BlockSpec(memory_space=pltpu.SMEM)
     dma = pltpu.SemaphoreType.DMA
-    cell_sems = pltpu.SemaphoreType.REGULAR((max(len(doubling(n_cell)), 1),))
-    grp_sems = pltpu.SemaphoreType.REGULAR((max(len(doubling((n_grp + 1) // 2)), 1),))
     effective, totals = pl.pallas_call(
         functools.partial(main_kernel, n_grp, n_cell, tiles, per, wide),
         out_shape=(
@@ -422,7 +381,7 @@
             pltpu.VMEM((species // wide, 2, wide), jnp.float32),
             pltpu.VMEM((devices, 2, wide), jnp.float32),
             dma((tiles // 2,)), dma((2,)), dma((2,)), dma((2,)), dma((2,)), dma((2,)), dma((2,)),
-            dma, dma, cell_sems, cell_sems, grp_sems, grp_sems,
+            dma, dma,
         ],
         compiler_params=pltpu.CompilerParams(
             collective_id=0, has_side_effects=True, vmem_limit_bytes=56 * 2**20

time: 43.4 us -> 35.7 us (0.82)
  Pallas kernels: 42.5 us -> 34.8 us
    pallas_call x1, Pallas kernels: 41.1 us -> 33.5 us  [per_device(): pl.pallas_call(functools.partial(main_kernel, n_grp, n_cell, tiles, per,...]
where the time goes in v2:
time: 35.7 us; the launch traced here: 35.5 us
  Pallas kernels  34.8 us (97%)
  between operations  0.64 us (2%)
    pallas_call x1, Pallas kernels, per_device(): pl.pallas_call(functools.partial(main_kernel, n_grp, n_cell, tiles, per,...  33.5 us
    pallas_call x1, Pallas kernels, per_device(): pl.pallas_call(close_kernel, out_shape=(jax.ShapeDtypeStruct((tiles, TILE...  1.31 us

profile of v2, /device:TPU:0, one launch (start us, length us, event | category | flops | bytes accessed | tf_op | source)
XLA Modules:
  0.0 35.5 jit_solution(1583026814065298660)
XLA Ops:
  0.6 33.5 %shard_map.59 = (f32[24,128]{1,0:T(8,128)}, f32[2,128]{1,0:T(2,128)}) custom-call(bf16[3072,4096]{1,0:T(8,128)(2,1)} %occ_hbm.1, bf16[24,128]{1,0:T(8,128)(2,1)} %bitcast.4, s32[4,24]{1,0:T(4,128)} %bitcast.5, s32[24]{0:T(128)} %cnt_ref.1), custom_call_target="tpu_custom_call" | custom-call | tf_op jit(solution)/shard_map/pallas_call | solution.py:362
  34.1 1.3 %shard_map.60 = (f32[24,128]{1,0:T(8,128)}, f32[1,128]{1,0:T(1,128)}) custom-call(f32[24,128]{1,0:T(8,128)} %get-tuple-element.6.eff_ref, f32[2,128]{1,0:T(2,128)} %get-tuple-element.7.tot_ref), custom_call_target="tpu_custom_call" | custom-call | tf_op jit(solution)/shard_map/pallas_call | solution.py:390

commit v3 on v2

v3 whole, which is shorter than its diff:
```python
import functools
import math

import jax
import jax.numpy as jnp
from jax import lax
from jax.experimental import pallas as pl
from jax.experimental.pallas import tpu as pltpu
from jax.sharding import PartitionSpec as P

sharpness = 40.0
epsilon = 1e-06

TILE = 128
PAIR = 2 * TILE
GROUP = 2
LEAD = 4
HALO_AT = 1
SCALE = sharpness * math.log2(math.e)


def gram_dot(a, b):
    return lax.dot_general(a, b, (((1,), (1,)), ((), ())), preferred_element_type=jnp.float32)


def fold_rows(x):
    return jnp.sum(x.reshape(x.shape[0] // 8, 8, x.shape[1]), axis=0)


def main_kernel(
    n_grp, n_cell, tiles, per, wide, occ_hbm, cond_hbm, nb_hbm, cnt_hbm, eff_hbm, per_hbm,
    cond_ref, nb_ref, cnt_ref, eff_ref, per_ref, small_sem,
    own, halo, gram, irow, icol, crow, ccol, chalo, acc, xin, xout, wl, sums, got,
    load_sem, halo_send, halo_recv, cond_send, cond_recv, acc_send, acc_recv,
    sum_send, sum_recv,
):
    rows = tiles * TILE
    pairs = tiles // 2
    species = own.shape[1]
    devices = n_grp * n_cell
    grp = lax.axis_index("grp")
    me = lax.axis_index("cell")
    rank = grp * n_cell + me
    first_tile = rank * tiles
    has_left = me > 0
    has_right = me < n_cell - 1
    left = (grp, jnp.maximum(me - 1, 0))
    right = (grp, jnp.minimum(me + 1, n_cell - 1))
    mesh_id = pl.DeviceIdType.MESH

    def load(k):
        start = k * PAIR if isinstance(k, int) else pl.multiple_of(k * PAIR, PAIR)
        return pltpu.make_async_copy(
            occ_hbm.at[pl.ds(start, PAIR)], own.at[pl.ds(start + PAIR, PAIR)], load_sem.at[k]
        )

    barrier = pltpu.get_barrier_semaphore()

    small = [
        pltpu.make_async_copy(cond_hbm, cond_ref, small_sem.at[0]),
        pltpu.make_async_copy(nb_hbm, nb_ref, small_sem.at[1]),
        pltpu.make_async_copy(cnt_hbm, cnt_ref, small_sem.at[2]),
    ]
    for copy in small:
        copy.start()
    for k in range(2):
        load(k).start()

    def greet(j, carry):
        other = lax.rem(rank + j, devices)
        pl.semaphore_signal(
            barrier, inc=1, device_id=(other // n_cell, lax.rem(other, n_cell)),
            device_id_type=mesh_id,
        )
        return carry

    lax.fori_loop(1, devices, greet, 0, unroll=True)

    for k in range(2, pairs):
        load(k).start()
    for copy in small:
        copy.wait()

    cond = cond_ref[...].astype(jnp.float32)
    for e in range(LEAD):
        crow[e] = jnp.zeros((8, TILE), jnp.float32)
    for t in range(tiles):
        crow[t + LEAD] = jnp.broadcast_to(cond[t : t + 1, :], (8, TILE))

    def remote(src, dst, send, recv, slot, target):
        return pltpu.make_async_remote_copy(
            src_ref=src, dst_ref=dst, send_sem=send.at[slot], recv_sem=recv.at[slot],
            device_id=target, device_id_type=mesh_id,
        )

    halo_r = remote(
        occ_hbm.at[pl.ds(rows - TILE, TILE)], halo.at[pl.ds(0, TILE)], halo_send, halo_recv, 0, right
    )
    halo_l = remote(
        occ_hbm.at[pl.ds(0, TILE)], halo.at[pl.ds(TILE, TILE)], halo_send, halo_recv, 1, left
    )
    last = LEAD + tiles - 1
    cond_r = remote(crow.at[last], chalo.at[0], cond_send, cond_recv, 0, right)
    cond_l = remote(crow.at[LEAD], chalo.at[1], cond_send, cond_recv, 1, left)
    acc_r = remote(xout.at[1], xin.at[0], acc_send, acc_recv, 0, right)
    acc_l = remote(xout.at[0], xin.at[1], acc_send, acc_recv, 1, left)

    def column(row8):
        return jnp.transpose(jnp.broadcast_to(row8[0:1, :], (TILE, TILE)))

    def hit(t, offset):
        at = jnp.maximum(t, 0)
        wanted = first_tile + at + offset
        found = jnp.int32(0)
        for s in range(nb_ref.shape[0]):
            same = jnp.logical_and(nb_ref[s, at] == wanted, s < cnt_ref[at])
            found = jnp.maximum(found, same.astype(jnp.int32))
        found = jnp.where(t >= 0, found, 0)
        return jnp.full((TILE, TILE), found, jnp.int32) > 0

    def paired(mask, value):
        return jnp.where(mask, value, 0.0)

    eye = lax.broadcasted_iota(jnp.int32, (TILE, TILE), 0) == lax.broadcasted_iota(
        jnp.int32, (TILE, TILE), 1
    )

    def part(slot, base, i, j):
        return gram[slot, base + i * TILE : base + (i + 1) * TILE, j * TILE : (j + 1) * TILE]

    def own_own(slot, base, k):
        e = 2 * k + LEAD
        near = hit(2 * k, 1)
        tiles_g = [[part(slot, base, i, j) for j in range(2)] for i in range(2)]
        rows_inv = []
        cols_inv = []
        for i in range(2):
            diag = jnp.sum(jnp.where(eye, tiles_g[i][i], 0.0), axis=0, keepdims=True)
            inv = jnp.broadcast_to(lax.rsqrt(diag + epsilon), (TILE, TILE))
            col = jnp.transpose(inv) * SCALE
            irow[e + i] = inv[0:8]
            icol[e + i] = col
            rows_inv.append(inv[0:1])
            cols_inv.append(col)
        cc = [column(crow[e]), column(crow[e + 1])]
        ccol[e] = cc[0]
        ccol[e + 1] = cc[1]
        w = [[None, None], [None, None]]
        for i in range(2):
            for j in range(2):
                v = jnp.exp2(tiles_g[i][j] * cols_inv[i] * rows_inv[j])
                w[i][j] = jnp.where(eye, 0.0, v) if i == j else paired(near, v)
        for j in range(2):
            acc[e + j, 0:8, :] = fold_rows(w[0][j] * cc[0] + w[1][j] * cc[1])
            acc[e + j, 8:16, :] = fold_rows(w[0][j] + w[1][j])

    def prev_own(slot, k):
        e = 2 * k + LEAD
        far0, near1, far1 = hit(2 * k - 2, 2), hit(2 * k - 1, 1), hit(2 * k - 1, 2)
        r0, r1 = irow[e, 0:1, :], irow[e + 1, 0:1, :]
        w00 = paired(far0, jnp.exp2(part(slot, 0, 0, 0) * icol[e - 2] * r0))
        w10 = paired(near1, jnp.exp2(part(slot, 0, 1, 0) * icol[e - 1] * r0))
        w11 = paired(far1, jnp.exp2(part(slot, 0, 1, 1) * icol[e - 1] * r1))
        cp0, cp1 = ccol[e - 2], ccol[e - 1]
        acc[e, 0:8, :] += fold_rows(w00 * cp0 + w10 * cp1)
        acc[e, 8:16, :] += fold_rows(w00 + w10)
        acc[e + 1, 0:8, :] += fold_rows(w11 * cp1)
        acc[e + 1, 8:16, :] += fold_rows(w11)
        c0, c1 = crow[e, 0:1, :], crow[e + 1, 0:1, :]
        acc[e - 2, 0:8, :] += fold_rows(jnp.transpose(w00 * c0))
        acc[e - 2, 8:16, :] += fold_rows(jnp.transpose(w00))
        acc[e - 1, 0:8, :] += fold_rows(jnp.transpose(w10 * c0 + w11 * c1))
        acc[e - 1, 8:16, :] += fold_rows(jnp.transpose(w10 + w11))

    def post(slot, k):
        own_own(slot, PAIR, k)
        prev_own(slot, k)

    def block(k, slot):
        start = pl.multiple_of(k * PAIR, PAIR)
        gram[slot] = gram_dot(own[pl.ds(start, 2 * PAIR), :], own[pl.ds(start + PAIR, PAIR), :])

    def send_halo():
        pl.semaphore_wait(barrier, devices - 1)

        @pl.when(has_right)
        def _():
            halo_r.start()
            cond_r.start()

        @pl.when(has_left)
        def _():
            halo_l.start()
            cond_l.start()

    @pl.when(jnp.logical_not(has_left))
    def _():
        halo[0:TILE, :] = jnp.zeros((TILE, species), halo.dtype)
        chalo[0] = jnp.zeros((8, TILE), jnp.float32)
        xin[0] = jnp.zeros((16, TILE), jnp.float32)

    @pl.when(jnp.logical_not(has_right))
    def _():
        halo[TILE:PAIR, :] = jnp.zeros((TILE, species), halo.dtype)
        chalo[1] = jnp.zeros((8, TILE), jnp.float32)
        xin[1] = jnp.zeros((16, TILE), jnp.float32)

    def step(i, carry):
        first = GROUP * i
        pl.when(i == HALO_AT)(send_halo)
        for u in range(GROUP):
            load(first + u).wait()
        for u in range(GROUP):
            block(first + u, u)
            post((u - 1) % GROUP, first + u - 1)
        return carry

    if HALO_AT < 0:
        send_halo()
    lax.fori_loop(0, pairs // GROUP, step, 0)
    @pl.when(has_left)
    def _():
        halo_r.wait_recv()
        cond_r.wait_recv()

    @pl.when(has_right)
    def _():
        halo_l.wait_recv()
        cond_l.wait_recv()

    def halo_inverse(side):
        total = jnp.zeros((TILE, TILE), jnp.float32)
        for q in range(species // TILE):
            x = halo[side * TILE : (side + 1) * TILE, q * TILE : (q + 1) * TILE]
            x = x.astype(jnp.float32)
            total = total + x * x
        inv = lax.rsqrt(jnp.sum(total, axis=1, keepdims=True) + epsilon)
        return jnp.transpose(jnp.broadcast_to(inv, (TILE, TILE)))

    post(GROUP - 1, pairs - 1)
    near_rows = jnp.concatenate(
        [own[PAIR : 2 * PAIR, :], own[rows : rows + TILE, :]], axis=0
    )
    edge = gram_dot(near_rows, halo[...])
    inv_l, inv_r = halo_inverse(0), halo_inverse(1)
    e0, e1, e22 = LEAD, LEAD + 1, LEAD + tiles - 2
    w0 = paired(hit(0, -1), jnp.exp2(edge[0:TILE, 0:TILE] * icol[e0] * inv_l))
    w1 = paired(hit(1, -2), jnp.exp2(edge[TILE:PAIR, 0:TILE] * icol[e1] * inv_l))
    w2 = paired(hit(tiles - 2, 2), jnp.exp2(edge[PAIR:, TILE:] * icol[e22] * inv_r))
    xout[0, 0:8, :] = fold_rows(w0 * ccol[e0] + w1 * ccol[e1])
    xout[0, 8:16, :] = fold_rows(w0 + w1)
    xout[1, 0:8, :] = fold_rows(w2 * ccol[e22])
    xout[1, 8:16, :] = fold_rows(w2)

    @pl.when(has_right)
    def _():
        acc_r.start()

    @pl.when(has_left)
    def _():
        acc_l.start()

    for e, w, side in ((e0, w0, 0), (e1, w1, 0), (e22, w2, 1)):
        acc[e, 0:8, :] += fold_rows(jnp.transpose(w * chalo[side, 0:1, :]))
        acc[e, 8:16, :] += fold_rows(jnp.transpose(w))

    line = lax.broadcasted_iota(jnp.int32, (16, TILE), 0)

    def finish(t, extra=None):
        e = t + LEAD
        total = acc[e]
        if extra is not None:
            total = total + xin[extra]
        numer = jnp.sum(total[0:8], axis=0, keepdims=True)
        denom = jnp.sum(total[8:16], axis=0, keepdims=True)
        eff = crow[e, 0:1, :] * numer / denom
        eff_ref[t : t + 1, :] = eff
        both = jnp.where(line == 0, eff, jnp.where(line == 1, 1.0, 0.0))
        wl[:, t * TILE : (t + 1) * TILE] = both.astype(jnp.bfloat16)

    for t in range(1, tiles - 1):
        finish(t)

    wide_step = 2048 if species % 2048 == 0 else TILE
    blocks = wide_step // TILE

    def inner(i, carry):
        cols = pl.ds(pl.multiple_of(i * wide_step, wide_step), wide_step)
        value = jnp.dot(
            wl[:, TILE : rows - TILE], own[PAIR + TILE : PAIR + rows - TILE, cols],
            preferred_element_type=jnp.float32,
        )
        for q in range(blocks):
            sums[i * blocks + q] = value[0:2, q * TILE : (q + 1) * TILE]
        return carry

    lax.fori_loop(0, species // wide_step, inner, 0)

    @pl.when(has_left)
    def _():
        acc_r.wait_recv()

    @pl.when(has_right)
    def _():
        acc_l.wait_recv()

    finish(0, 0)
    finish(tiles - 1, 1)

    eff_copy = pltpu.make_async_copy(eff_ref, eff_hbm, small_sem.at[0])
    eff_copy.start()
    share = wide // per

    chunks = species // wide_step

    def outer(i, carry):
        chunk = lax.rem(i + rank // (blocks * share) + chunks // 2, chunks)
        cols = pl.ds(pl.multiple_of(chunk * wide_step, wide_step), wide_step)
        ends = [own[PAIR : PAIR + TILE, cols], own[PAIR + rows - TILE : PAIR + rows, cols]]
        value = jnp.dot(
            jnp.concatenate([wl[:, 0:TILE], wl[:, rows - TILE : rows]], axis=1),
            jnp.concatenate(ends, axis=0), preferred_element_type=jnp.float32,
        )
        for q in range(blocks):
            sums[chunk * blocks + q] += value[0:2, q * TILE : (q + 1) * TILE]
        for q in range(blocks * share):
            owner = chunk * blocks * share + lax.rem(rank + q + blocks * share // 2, blocks * share)

            @pl.when(owner != rank)
            def _():
                pltpu.make_async_remote_copy(
                    src_ref=sums.at[owner // share],
                    dst_ref=got.at[lax.rem(rank - owner + devices, devices)],
                    send_sem=sum_send, recv_sem=sum_recv,
                    device_id=(owner // n_cell, lax.rem(owner, n_cell)), device_id_type=mesh_id,
                ).start()

        return carry

    lax.fori_loop(0, species // wide_step, outer, 0)
    got[0] = sums[rank // share]
    others = got.at[pl.ds(1, devices - 1)]
    pltpu.make_async_copy(others, others, sum_recv).wait()
    total = jnp.sum(got[...], axis=0)
    per_ref[...] = jnp.sqrt(jnp.sqrt(total[0:1, :] / total[1:2, :]))
    per_copy = pltpu.make_async_copy(per_ref, per_hbm, small_sem.at[1])
    per_copy.start()
    pltpu.make_async_copy(others, others, sum_send).wait()

    @pl.when(has_right)
    def _():
        halo_r.wait_send()
        cond_r.wait_send()
        acc_r.wait_send()

    @pl.when(has_left)
    def _():
        halo_l.wait_send()
        cond_l.wait_send()
        acc_l.wait_send()

    eff_copy.wait()
    per_copy.wait()


def close_kernel(eff_ref, per_ref, eff_out, per_out, sem):
    copies = [
        pltpu.make_async_copy(eff_ref, eff_out, sem.at[0]),
        pltpu.make_async_copy(per_ref, per_out, sem.at[1]),
    ]
    for copy in copies:
        copy.start()
    for copy in copies:
        copy.wait()


def per_device(n_grp, n_cell, occurrence, condition, neighbours, pair_count):
    tiles = pair_count.shape[0]
    rows, species = occurrence.shape
    devices = n_grp * n_cell
    per = species // devices
    wide = max(per, TILE)
    whole = pl.BlockSpec(memory_space=pl.ANY)
    dma = pltpu.SemaphoreType.DMA
    effective, persistence = pl.pallas_call(
        functools.partial(main_kernel, n_grp, n_cell, tiles, per, wide),
        out_shape=(
            jax.ShapeDtypeStruct((tiles, TILE), jnp.float32),
            jax.ShapeDtypeStruct((1, wide), jnp.float32),
        ),
        in_specs=[whole] * 4,
        out_specs=(whole, whole),
        scratch_shapes=[
            pltpu.VMEM((tiles, TILE), jnp.bfloat16),
            pltpu.SMEM((neighbours.shape[1], tiles), jnp.int32),
            pltpu.SMEM((tiles,), jnp.int32),
            pltpu.VMEM((tiles, TILE), jnp.float32),
            pltpu.VMEM((1, wide), jnp.float32),
            dma((3,)),
            pltpu.VMEM((PAIR + rows, species), jnp.bfloat16),
            pltpu.VMEM((PAIR, species), jnp.bfloat16),
            pltpu.VMEM((GROUP, 2 * PAIR, PAIR), jnp.float32),
            pltpu.VMEM((LEAD + tiles, 8, TILE), jnp.float32),
            pltpu.VMEM((LEAD + tiles, TILE, TILE), jnp.float32),
            pltpu.VMEM((LEAD + tiles, 8, TILE), jnp.float32),
            pltpu.VMEM((LEAD + tiles, TILE, TILE), jnp.float32),
            pltpu.VMEM((2, 8, TILE), jnp.float32),
            pltpu.VMEM((LEAD + tiles, 16, TILE), jnp.float32),
            pltpu.VMEM((2, 16, TILE), jnp.float32),
            pltpu.VMEM((2, 16, TILE), jnp.float32),
            pltpu.VMEM((16, rows), jnp.bfloat16),
            pltpu.VMEM((species // wide, 2, wide), jnp.float32),
            pltpu.VMEM((devices, 2, wide), jnp.float32),
            dma((tiles // 2,)), dma((2,)), dma((2,)), dma((2,)), dma((2,)), dma((2,)), dma((2,)),
            dma, dma,
        ],
        compiler_params=pltpu.CompilerParams(
            collective_id=0, has_side_effects=True, vmem_limit_bytes=56 * 2**20
        ),
    )(occurrence, condition.reshape(tiles, TILE), neighbours.T, pair_count)
    effective, persistence = pl.pallas_call(
        close_kernel,
        out_shape=(
            jax.ShapeDtypeStruct((tiles, TILE), jnp.float32),
            jax.ShapeDtypeStruct((1, wide), jnp.float32),
        ),
        in_specs=[whole] * 2,
        out_specs=(whole, whole),
        scratch_shapes=[dma((2,))],
    )(effective, persistence)
    persistence = persistence.reshape(wide)
    if per < wide:
        offset = lax.rem(lax.axis_index(("grp", "cell")) * per, wide)
        persistence = lax.dynamic_slice_in_dim(persistence, offset, per)
    return effective.reshape(rows), persistence


def solution(mesh):
    return jax.shard_map(
        functools.partial(per_device, mesh.shape["grp"], mesh.shape["cell"]),
        mesh=mesh,
        in_specs=(
            P(("grp", "cell"), None),
            P(("grp", "cell")),
            P(("grp", "cell"), None),
            P(("grp", "cell")),
        ),
        out_specs=(P(("grp", "cell")), P(("grp", "cell"))),
        check_vma=False,
    )
```

time: 35.7 us -> 34.5 us (0.966)
  Pallas kernels: 34.8 us -> 33.7 us
    pallas_call x1, Pallas kernels: 33.5 us -> 32.2 us  [per_device(): pl.pallas_call(functools.partial(main_kernel, n_grp, n_cell, tiles, per,...]
where the time goes in v3:
time: 34.5 us; the launch traced here: 34.3 us
  Pallas kernels  33.7 us (98%)
  between operations  0.64 us (2%)
    pallas_call x1, Pallas kernels, per_device(): pl.pallas_call(functools.partial(main_kernel, n_grp, n_cell, tiles, per,...  32.2 us
    pallas_call x1, Pallas kernels, per_device(): pl.pallas_call(close_kernel, out_shape=(jax.ShapeDtypeStruct((tiles, TILE...  1.51 us

profile of v3, /device:TPU:0, one launch (start us, length us, event | category | flops | bytes accessed | tf_op | source)
XLA Modules:
  0.0 34.3 jit_solution(11195691613147641495)
XLA Ops:
  0.6 32.2 %shard_map.59 = (f32[24,128]{1,0:T(8,128)}, f32[1,128]{1,0:T(1,128)}) custom-call(bf16[3072,4096]{1,0:T(8,128)(2,1)} %occ_hbm.1, bf16[24,128]{1,0:T(8,128)(2,1)} %bitcast.4, s32[4,24]{1,0:T(4,128)} %bitcast.5, s32[24]{0:T(128)} %cnt_hbm.1), custom_call_target="tpu_custom_call" | custom-call | tf_op jit(solution)/shard_map/pallas_call | solution.py:385
  32.8 1.5 %shard_map.60 = (f32[24,128]{1,0:T(8,128)}, f32[1,128]{1,0:T(1,128)}) custom-call(f32[24,128]{1,0:T(8,128)} %get-tuple-element.6.eff_ref, f32[1,128]{1,0:T(1,128)} %get-tuple-element.7.per_ref), custom_call_target="tpu_custom_call" | custom-call | tf_op jit(solution)/shard_map/pallas_call | solution.py:421

commit v4 on v3

--- a/solution.py
+++ b/solution.py
@@ -28,8 +28,8 @@
 
 
 def main_kernel(
-    n_grp, n_cell, tiles, per, wide, occ_hbm, cond_hbm, nb_hbm, cnt_hbm, eff_hbm, per_hbm,
-    cond_ref, nb_ref, cnt_ref, eff_ref, per_ref, small_sem,
+    n_grp, n_cell, tiles, per, wide, occ_hbm, cond_hbm, nb_hbm, cnt_hbm, eff_ref, per_ref,
+    cond_ref, nb_ref, cnt_ref, small_sem,
     own, halo, gram, irow, icol, crow, ccol, chalo, acc, xin, xout, wl, sums, got,
     load_sem, halo_send, halo_recv, cond_send, cond_recv, acc_send, acc_recv,
     sum_send, sum_recv,
@@ -307,8 +307,6 @@
     finish(0, 0)
     finish(tiles - 1, 1)
 
-    eff_copy = pltpu.make_async_copy(eff_ref, eff_hbm, small_sem.at[0])
-    eff_copy.start()
     share = wide // per
 
     chunks = species // wide_step
@@ -343,8 +341,6 @@
     pltpu.make_async_copy(others, others, sum_recv).wait()
     total = jnp.sum(got[...], axis=0)
     per_ref[...] = jnp.sqrt(jnp.sqrt(total[0:1, :] / total[1:2, :]))
-    per_copy = pltpu.make_async_copy(per_ref, per_hbm, small_sem.at[1])
-    per_copy.start()
     pltpu.make_async_copy(others, others, sum_send).wait()
 
     @pl.when(has_right)
@@ -358,20 +354,6 @@
         halo_l.wait_send()
         cond_l.wait_send()
         acc_l.wait_send()
-
-    eff_copy.wait()
-    per_copy.wait()
-
-
-def close_kernel(eff_ref, per_ref, eff_out, per_out, sem):
-    copies = [
-        pltpu.make_async_copy(eff_ref, eff_out, sem.at[0]),
-        pltpu.make_async_copy(per_ref, per_out, sem.at[1]),
-    ]
-    for copy in copies:
-        copy.start()
-    for copy in copies:
-        copy.wait()
 
 
 def per_device(n_grp, n_cell, occurrence, condition, neighbours, pair_count):
@@ -381,21 +363,20 @@
     per = species // devices
     wide = max(per, TILE)
     whole = pl.BlockSpec(memory_space=pl.ANY)
+    vmem = pl.BlockSpec(memory_space=pltpu.VMEM)
     dma = pltpu.SemaphoreType.DMA
     effective, persistence = pl.pallas_call(
         functools.partial(main_kernel, n_grp, n_cell, tiles, per, wide),
         out_shape=(
-            jax.ShapeDtypeStruct((tiles, TILE), jnp.float32),
-            jax.ShapeDtypeStruct((1, wide), jnp.float32),
+            pltpu.VMEM((tiles, TILE), jnp.float32),
+            pltpu.VMEM((1, wide), jnp.float32),
         ),
         in_specs=[whole] * 4,
-        out_specs=(whole, whole),
+        out_specs=(vmem, vmem),
         scratch_shapes=[
             pltpu.VMEM((tiles, TILE), jnp.bfloat16),
             pltpu.SMEM((neighbours.shape[1], tiles), jnp.int32),
             pltpu.SMEM((tiles,), jnp.int32),
-            pltpu.VMEM((tiles, TILE), jnp.float32),
-            pltpu.VMEM((1, wide), jnp.float32),
             dma((3,)),
             pltpu.VMEM((PAIR + rows, species), jnp.bfloat16),
             pltpu.VMEM((PAIR, species), jnp.bfloat16),
@@ -418,16 +399,6 @@
             collective_id=0, has_side_effects=True, vmem_limit_bytes=56 * 2**20
         ),
     )(occurrence, condition.reshape(tiles, TILE), neighbours.T, pair_count)
-    effective, persistence = pl.pallas_call(
-        close_kernel,
-        out_shape=(
-            jax.ShapeDtypeStruct((tiles, TILE), jnp.float32),
-            jax.ShapeDtypeStruct((1, wide), jnp.float32),
-        ),
-        in_specs=[whole] * 2,
-        out_specs=(whole, whole),
-        scratch_shapes=[dma((2,))],
-    )(effective, persistence)
     persistence = persistence.reshape(wide)
     if per < wide:
         offset = lax.rem(lax.axis_index(("grp", "cell")) * per, wide)

time: 34.5 us -> 33.7 us (0.977)
  Pallas kernels: 33.7 us -> 31.8 us
  local copies, waits for them, and re-layouts: 0 us -> 1.11 us
    pallas_call x1 -> x0, Pallas kernels: 1.51 us -> none  [per_device(): pl.pallas_call(close_kernel, out_shape=(jax.ShapeDtypeStruct((tiles, TILE...]
    unnamed x0 -> x2, local copies, waits for them, and re-layouts: none -> 1.11 us
    pallas_call x1, Pallas kernels: 32.2 us -> 31.8 us  [per_device(): pl.pallas_call(functools.partial(main_kernel, n_grp, n_cell, tiles, per,...]
where the time goes in v4:
time: 33.7 us; the launch traced here: 33.5 us
  Pallas kernels  31.8 us (94%)
  local copies, waits for them, and re-layouts  1.11 us (3%)
  between operations  0.64 us (2%)
    pallas_call x1, Pallas kernels, per_device(): pl.pallas_call(functools.partial(main_kernel, n_grp, n_cell, tiles, per,...  31.8 us
    unnamed x2, local copies, waits for them, and re-layouts  1.11 us

profile of v4, /device:TPU:0, one launch (start us, length us, event | category | flops | bytes accessed | tf_op | source)
XLA Modules:
  0.0 33.5 jit_solution(13373702303875933035)
XLA Ops:
  0.6 31.8 %shard_map.59 = (f32[24,128]{1,0:T(8,128)S(1)}, f32[1,128]{1,0:T(1,128)S(1)}) custom-call(bf16[3072,4096]{1,0:T(8,128)(2,1)} %occ_hbm.1, bf16[24,128]{1,0:T(8,128)(2,1)} %bitcast.6, s32[4,24]{1,0:T(4,128)} %bitcast.7, s32[24]{0:T(128)} %cnt_hbm.1), custom_call_target="tpu_custom_call" | custom-call | tf_op jit(solution)/shard_map/pallas_call | solution.py:368
  32.4 0.6 %copy.8 = f32[3072]{0:T(1024)} copy(f32[3072]{0:T(1024)S(1)} %bitcast.4) | data formatting | bytes 24576
  33.0 0.5 %copy.9 = f32[128]{0:T(128)} copy(f32[128]{0:T(128)S(1)} %bitcast.5) | data formatting | bytes 1024

commit v5 on v4

--- a/solution.py
+++ b/solution.py
@@ -15,7 +15,6 @@
 PAIR = 2 * TILE
 GROUP = 2
 LEAD = 4
-HALO_AT = 1
 SCALE = sharpness * math.log2(math.e)
 
 
@@ -177,7 +176,7 @@
         prev_own(slot, k)
 
     def block(k, slot):
-        start = pl.multiple_of(k * PAIR, PAIR)
+        start = k * PAIR if isinstance(k, int) else pl.multiple_of(k * PAIR, PAIR)
         gram[slot] = gram_dot(own[pl.ds(start, 2 * PAIR), :], own[pl.ds(start + PAIR, PAIR), :])
 
     def send_halo():
@@ -206,8 +205,7 @@
         xin[1] = jnp.zeros((16, TILE), jnp.float32)
 
     def step(i, carry):
-        first = GROUP * i
-        pl.when(i == HALO_AT)(send_halo)
+        first = 2 + GROUP * i
         for u in range(GROUP):
             load(first + u).wait()
         for u in range(GROUP):
@@ -215,9 +213,13 @@
             post((u - 1) % GROUP, first + u - 1)
         return carry
 
-    if HALO_AT < 0:
-        send_halo()
-    lax.fori_loop(0, pairs // GROUP, step, 0)
+    load(0).wait()
+    gram[0, PAIR:, :] = gram_dot(own[PAIR : 2 * PAIR, :], own[PAIR : 2 * PAIR, :])
+    send_halo()
+    load(1).wait()
+    block(1, 1)
+    own_own(0, PAIR, 0)
+    lax.fori_loop(0, (pairs - 2) // GROUP, step, 0)
     @pl.when(has_left)
     def _():
         halo_r.wait_recv()

time: 33.7 us -> 33.5 us (level)
  no operation moved by 1% of the time
where the time goes in v5:
time: 33.5 us; the launch traced here: 33.3 us
  Pallas kernels  31.5 us (94%)
  local copies, waits for them, and re-layouts  1.11 us (3%)
  between operations  0.64 us (2%)
    pallas_call x1, Pallas kernels, per_device(): pl.pallas_call(functools.partial(main_kernel, n_grp, n_cell, tiles, per,...  31.5 us
    unnamed x2, local copies, waits for them, and re-layouts  1.11 us

profile of v5, /device:TPU:0, one launch (start us, length us, event | category | flops | bytes accessed | tf_op | source)
XLA Modules:
  0.0 33.3 jit_solution(11550226957099801375)
XLA Ops:
  0.6 31.5 %shard_map.59 = (f32[24,128]{1,0:T(8,128)S(1)}, f32[1,128]{1,0:T(1,128)S(1)}) custom-call(bf16[3072,4096]{1,0:T(8,128)(2,1)} %occ_hbm.1, bf16[24,128]{1,0:T(8,128)(2,1)} %bitcast.6, s32[4,24]{1,0:T(4,128)} %bitcast.7, s32[24]{0:T(128)} %cnt_hbm.1), custom_call_target="tpu_custom_call" | custom-call | tf_op jit(solution)/shard_map/pallas_call | solution.py:370
  32.2 0.6 %copy.8 = f32[3072]{0:T(1024)} copy(f32[3072]{0:T(1024)S(1)} %bitcast.4) | data formatting | bytes 24576
  32.8 0.5 %copy.9 = f32[128]{0:T(128)} copy(f32[128]{0:T(128)S(1)} %bitcast.5) | data formatting | bytes 1024

commit v6 on v5

--- a/solution.py
+++ b/solution.py
@@ -27,8 +27,8 @@
 
 
 def main_kernel(
-    n_grp, n_cell, tiles, per, wide, occ_hbm, cond_hbm, nb_hbm, cnt_hbm, eff_ref, per_ref,
-    cond_ref, nb_ref, cnt_ref, small_sem,
+    n_grp, n_cell, tiles, per, wide, occ_hbm, cond_ref, nb_hbm, cnt_hbm, eff_ref, per_ref,
+    nb_ref, cnt_ref, small_sem,
     own, halo, gram, irow, icol, crow, ccol, chalo, acc, xin, xout, wl, sums, got,
     load_sem, halo_send, halo_recv, cond_send, cond_recv, acc_send, acc_recv,
     sum_send, sum_recv,
@@ -56,7 +56,6 @@
     barrier = pltpu.get_barrier_semaphore()
 
     small = [
-        pltpu.make_async_copy(cond_hbm, cond_ref, small_sem.at[0]),
         pltpu.make_async_copy(nb_hbm, nb_ref, small_sem.at[1]),
         pltpu.make_async_copy(cnt_hbm, cnt_ref, small_sem.at[2]),
     ]
@@ -373,10 +372,9 @@
             pltpu.VMEM((tiles, TILE), jnp.float32),
             pltpu.VMEM((1, wide), jnp.float32),
         ),
-        in_specs=[whole] * 4,
+        in_specs=[whole, vmem, whole, whole],
         out_specs=(vmem, vmem),
         scratch_shapes=[
-            pltpu.VMEM((tiles, TILE), jnp.bfloat16),
             pltpu.SMEM((neighbours.shape[1], tiles), jnp.int32),
             pltpu.SMEM((tiles,), jnp.int32),
             dma((3,)),

time: 33.5 us -> 34 us (1.015)
  Pallas kernels: 31.5 us -> 32 us
    pallas_call x1, Pallas kernels: 31.5 us -> 32 us  [per_device(): pl.pallas_call(functools.partial(main_kernel, n_grp, n_cell, tiles, per,...]
where the time goes in v6:
time: 34 us; the launch traced here: 33.8 us
  Pallas kernels  32 us (94%)
  local copies, waits for them, and re-layouts  1.11 us (3%)
  between operations  0.64 us (2%)
    pallas_call x1, Pallas kernels, per_device(): pl.pallas_call(functools.partial(main_kernel, n_grp, n_cell, tiles, per,...  32 us
    unnamed x2, local copies, waits for them, and re-layouts  1.11 us

profile of v6, /device:TPU:0, one launch (start us, length us, event | category | flops | bytes accessed | tf_op | source)
XLA Modules:
  0.0 33.8 jit_solution(17233748100872986410)
XLA Ops:
  0.6 32.0 %shard_map.59 = (f32[24,128]{1,0:T(8,128)S(1)}, f32[1,128]{1,0:T(1,128)S(1)}) custom-call(bf16[3072,4096]{1,0:T(8,128)(2,1)} %occ_hbm.1, bf16[24,128]{1,0:T(8,128)(2,1)} %bitcast.6, s32[4,24]{1,0:T(4,128)} %bitcast.7, s32[24]{0:T(128)} %cnt_hbm.1), custom_call_target="tpu_custom_call" | custom-call | tf_op jit(solution)/shard_map/pallas_call | solution.py:369
  32.6 0.6 %copy.8 = f32[3072]{0:T(1024)} copy(f32[3072]{0:T(1024)S(1)} %bitcast.4) | data formatting | bytes 24576
  33.2 0.5 %copy.9 = f32[128]{0:T(128)} copy(f32[128]{0:T(128)S(1)} %bitcast.5) | data formatting | bytes 1024
